TPU v7x, 32 devices: a whole 2x2x4 slice. The times are simulated.
32 devices in a mesh: grp: 8 (over z, x), fsdp: 4 (over y, core).
Axes of the slice: x: 2, y: 2, z: 4, core: 2. Of those that a mesh axis runs over, the one named last changes fastest.
Arguments:
- text: bfloat16 [4096, 8192], P(('grp', 'fsdp'))
- vision: bfloat16 [512, 8192], P(('grp', 'fsdp'))
- vision_token: int32 [512], P(('grp', 'fsdp')), may hold values from 0 to 4095, as said below
- gain: bfloat16 [8192], P('fsdp'), may hold values from 0.099609375 to 1.8984375
- cotangent: bfloat16 [4096, 8192], P(('grp', 'fsdp')), may hold values from -6 to 6
Outputs:
- vision_grad: bfloat16 [512, 8192], P(('grp', 'fsdp'))
- gain_grad: float32 [8192], P('fsdp')
Inputs may be any that keep to these rules, and one draw needn't show every extreme that they name: `vision_token`: device d of the flattened grp+fsdp order holds vision rows d * 16 to (d + 1) * 16 - 1 and token rows d * 128 to (d + 1) * 128 - 1. The rows held in group g go to tokens of group (g + 2) mod 8; a device sends at most 4 rows to any one device, and in every group some device receives exactly 4 rows from every device of its source group. No token receives two rows.
All inputs are finite; a program needn't handle non-finite values.
Results may differ from a plain program's by a relative error of at most 0.001.
Values may be sent and summed in bfloat16 or wider, within the bound.
A program may use at most 64 MiB of HBM per device.

v0:
```python
import jax
import jax.numpy as jnp
from jax import lax
from jax.sharding import PartitionSpec as P


def shifted(value, axis, steps):
    count = lax.axis_size(axis)
    pairs = [(source, (source + steps) % count) for source in range(count)]
    return lax.ppermute(value, axis, pairs)


def slot_order(target, groups, capacity):
    onehot = (target[:, None] == jnp.arange(groups)[None, :]).astype(jnp.int32)
    rank = jnp.sum((jnp.cumsum(onehot, axis=0) - 1) * onehot, axis=1)
    return target * capacity + rank


def norm_backward(values, upper, full_gain):
    inv = lax.rsqrt(jnp.mean(values * values, axis=-1, keepdims=True) + 1e-06)
    scaled = upper * full_gain
    inner = jnp.mean(values * scaled, axis=-1, keepdims=True)
    token_grad = (inv * scaled - values * inv * inv * inv * inner).astype(jnp.bfloat16)
    return (token_grad, upper * values * inv)


def shards(text, vision, vision_token, gain, cotangent):
    groups = lax.axis_size("fsdp")
    hop = lax.axis_size("grp") // 4
    tok_dev, width = text.shape
    capacity = vision.shape[0] // 4
    local = vision_token % tok_dev
    target = vision_token // tok_dev % groups
    full_gain = lax.all_gather(gain, "fsdp", axis=0, tiled=True).astype(jnp.float32)
    moved_local, moved_target = shifted((local, target), "grp", hop)
    slot = slot_order(moved_target, groups, capacity)
    places = jnp.full((groups * capacity,), tok_dev, jnp.int32).at[slot].set(moved_local)
    arrived_places = lax.all_to_all(
        places.reshape(groups, capacity), "fsdp", split_axis=0, concat_axis=0, tiled=True
    )
    arrived_places = arrived_places.reshape(groups * capacity)
    marks = jnp.zeros((tok_dev,), jnp.float32).at[arrived_places].set(1.0, mode="drop")
    values = text.astype(jnp.float32)
    upper = cotangent.astype(jnp.float32)
    inv = lax.rsqrt(jnp.mean(values * values, axis=-1, keepdims=True) + 1e-06)
    text_terms = jnp.sum(upper * values * inv * (1.0 - marks)[:, None], axis=0)
    asked = jnp.take(cotangent, jnp.minimum(arrived_places, tok_dev - 1), axis=0)
    asked = asked.reshape(groups, capacity, width)
    returned = lax.all_to_all(asked, "fsdp", split_axis=0, concat_axis=0, tiled=True).reshape(
        groups * capacity, width
    )
    own_cot = shifted(returned[slot], "grp", -hop)
    vision_grad, vision_terms = norm_backward(
        vision.astype(jnp.float32), own_cot.astype(jnp.float32), full_gain
    )
    terms = text_terms + jnp.sum(vision_terms, axis=0)
    share_width = width // groups
    total = lax.psum(terms, ("grp", "fsdp"))
    gain_grad = lax.dynamic_slice_in_dim(total, lax.axis_index("fsdp") * share_width, share_width)
    return (vision_grad, gain_grad)


def solution(mesh):
    return jax.shard_map(
        shards,
        mesh=mesh,
        in_specs=(
            P(("grp", "fsdp"), None),
            P(("grp", "fsdp"), None),
            P(("grp", "fsdp")),
            P("fsdp"),
            P(("grp", "fsdp"), None),
        ),
        out_specs=(P(("grp", "fsdp"), None), P("fsdp")),
        check_vma=False,
    )
```

profile of v0, /device:TPU:0, one launch (start us, length us, event | category | flops | bytes accessed | tf_op | source)
XLA Modules:
  0.0 84.6 jit_solution(9794965567442006342)
XLA Ops:
  0.6 0.0 copy-start
  0.6 0.8 and_select_fusion
  1.5 3.1 %collective-permute-start = (s32[16]{0:T(128)S(1)}, s32[16]{0:T(128)S(1)}, u32[]{:S(2)}, u32[]{:S(2)}) collective-permute-start(s32[16]{0:T(128)S(1)} %get-tuple-element.9), channel_id=1, source_target_pairs={{0,8},{4,12},{8,16},{12,20},{16,24},{20,28},{24,0},{28,4},{1,9},{5... | collective-permute-start | bytes 200 | tf_op jit(solution)/shard_map/ppermute | solution.py:10
  4.5 1.6 %collective-permute-start.1 = (s32[16]{0:T(128)S(1)}, s32[16]{0:T(128)S(1)}, u32[]{:S(2)}, u32[]{:S(2)}) collective-permute-start(s32[16]{0:T(128)S(1)} %get-tuple-element.8), channel_id=1, source_target_pairs={{0,8},{4,12},{8,16},{12,20},{16,24},{20,28},{24,0},{28,4},{1,9},{5... | collective-permute-start | bytes 200 | tf_op jit(solution)/shard_map/ppermute | solution.py:10
  6.1 5.3 %all_gather.3 = bf16[8192]{0:T(1024)(128)(2,1)S(1)} all-gather(bf16[2048]{0:T(1024)(128)(2,1)} %param.8), channel_id=1, replica_groups=mesh['grp'=8,'fsdp'=4] {'fsdp'}, dimensions={0}, use_global_device_ids=true | all-gather | bytes 20480 | tf_op jit(solution)/shard_map/all_gather | solution.py:34
  11.4 1.1 %fusion.7 = f32[16]{0:T(128)S(1)} fusion(bf16[16,8192]{1,0:T(8,128)(2,1)} %param.6), kind=kLoop, calls=%fused_computation.18 | loop fusion | flops 393200 | bytes 262208 | tf_op jit(solution)/shard_map/reduce_sum | solution.py:20
  12.6 2.1 %fusion.3 = f32[128]{0:T(128)S(1)} fusion(bf16[128,8192]{1,0:T(8,128)(2,1)} %param.5), kind=kLoop, calls=%fused_computation.9 | loop fusion | flops 3145600 | bytes 2097664 | tf_op jit(solution)/shard_map/reduce_sum | solution.py:45
  14.6 0.0 collective-permute-done
  14.7 0.1 fusion.14
  14.8 0.2 select_reduce_fusion
  15.0 0.0 collective-permute-done.1
  15.0 0.6 scatter_custom_fusion
  15.6 0.1 all_to_all.9
  15.7 6.3 %all_to_all.14 = s32[4,1,4]{2,1,0:T(1,128)S(1)} all-to-all(s32[4,1,4]{2,1,0:T(1,128)S(1)} %bitcast.7), channel_id=1, replica_groups=mesh['grp'=8,'fsdp'=4] {'fsdp'}, dimensions={0} | all-to-all | bytes 128 | tf_op jit(solution)/shard_map/all_to_all | solution.py:38
  22.0 0.5 broadcast.201
  22.5 0.7 broadcast_minimum_fusion
  23.2 0.1 reshape.102
  23.3 0.0 copy-done
  23.3 0.7 gather_fusion
  24.0 0.1 gather.10
  24.2 0.9 %broadcast_select_fusion = bf16[4,4,8192]{2,1,0:T(4,128)(2,1)} fusion(bf16[4,4,8192]{2,1,0:T(4,128)(2,1)S(1)} %gather.10, pred[4,4]{1,0:T(4,128)(4,1)S(1)} %compare_and_fusion), kind=kLoop, calls=%fused_computation.25 | loop fusion | flops 131072 | bytes 524304 | tf_op jit(solution)/shard_map/jit(_take)/select_n | solution.py:47
  25.0 3.4 %all-to-all-start.1 = ((bf16[4,4,8192]{2,1,0:T(4,128)(2,1)}), bf16[4,4,8192]{2,1,0:T(4,128)(2,1)S(1)}, u32[]{:S(2)}, u32[]{:S(2)}) async-start(bf16[4,4,8192]{2,1,0:T(4,128)(2,1)} %broadcast_select_fusion), calls=%async_computation.1 | async-start | bytes 524288 | tf_op jit(solution)/shard_map/all_to_all | solution.py:49
  28.5 0.6 scatter_custom_fusion.1
  29.1 5.3 %all-to-all-done.1 = bf16[4,4,8192]{2,1,0:T(4,128)(2,1)S(1)} async-done(((bf16[4,4,8192]{2,1,0:T(4,128)(2,1)}), bf16[4,4,8192]{2,1,0:T(4,128)(2,1)S(1)}, u32[]{:S(2)}, u32[]{:S(2)}) %all-to-all-start.1) | async-done | bytes 262176 | tf_op jit(solution)/shard_map/all_to_all | solution.py:49
  34.5 0.1 reshape.103
  34.5 0.7 gather_fusion.1
  35.2 2.3 %collective-permute-start.2 = (bf16[16,8192]{1,0:T(8,128)(2,1)S(1)}, bf16[16,8192]{1,0:T(8,128)(2,1)S(1)}, u32[]{:S(2)}, u32[]{:S(2)}) collective-permute-start(bf16[16,8192]{1,0:T(8,128)(2,1)S(1)} %gather_fusion.1), channel_id=1, source_target_pairs={{0,24},{4,28},{8,0},{12,4},{16,8},{20,12},{24,16},{28,20},{1,25},{... | collective-permute-start | bytes 786440 | tf_op jit(solution)/shard_map/ppermute | solution.py:10
  37.5 0.0 copy-start.1
  37.5 2.5 %fusion.2 = f32[8192]{0:T(1024)S(1)} fusion(bf16[128,8192]{1,0:T(8,128)(2,1)} %param.5, bf16[128,8192]{1,0:T(8,128)(2,1)S(1)} %copy-done, f32[128]{0:T(128)S(1)} %get-tuple-element.11, f32[128]{0:T(128)S(1)} %get-tuple-element.10), kind=kLoop, calls=%fused_computation.8 | loop fusion | flops 6283264 | bytes 4228096 | tf_op jit(solution)/shard_map/reduce_sum | solution.py:46
  40.1 3.1 %collective-permute-done.2 = bf16[16,8192]{1,0:T(8,128)(2,1)S(1)} collective-permute-done((bf16[16,8192]{1,0:T(8,128)(2,1)S(1)}, bf16[16,8192]{1,0:T(8,128)(2,1)S(1)}, u32[]{:S(2)}, u32[]{:S(2)}) %collective-permute-start.2) | collective-permute-done | bytes 262176 | tf_op jit(solution)/shard_map/ppermute | solution.py:10
  43.1 0.0 copy-done.1
  43.1 0.3 fusion.13
  43.5 39.6 %psum.7 = f32[8192]{0:T(1024)S(1)} all-reduce(f32[8192]{0:T(1024)S(1)} %add.82), channel_id=1, replica_groups=mesh['grp'=8,'fsdp'=4] {'grp','fsdp'}, use_global_device_ids=true, to_apply=%region_9.10 | all-reduce | flops 8192 | bytes 65536 | tf_op jit(solution)/shard_map/psum | solution.py:58
  83.1 0.6 dynamic_slice.3
  83.7 0.9 %fusion.6 = bf16[16,8192]{1,0:T(8,128)(2,1)} fusion(bf16[16,8192]{1,0:T(8,128)(2,1)S(1)} %collective-permute-done.2, bf16[16,8192]{1,0:T(8,128)(2,1)S(1)} %copy-done.1, f32[16]{0:T(128)S(1)} %broadcast_multiply_fusion, f32[8192]{0:T(1024)S(1)} %convert_element_type.24, f32[16]{0:T(128)S(1)} %add_rsqrt_fusion.1), kind=kLoop, calls=%fused_computation.17 | loop fusion | flops 1310720 | bytes 819328 | tf_op jit(solution)/shard_map/convert_element_type | solution.py:23
  (12 shorter events, 0.1 us)
Async XLA Ops:
  0.6 22.7 %copy-start = (bf16[128,8192]{1,0:T(8,128)(2,1)S(1)}, bf16[128,8192]{1,0:T(8,128)(2,1)}, u32[]{:S(2)}) copy-start(bf16[128,8192]{1,0:T(8,128)(2,1)} %param.9) | copy-start | bytes 6291460
  1.5 13.2 %collective-permute-start = (s32[16]{0:T(128)S(1)}, s32[16]{0:T(128)S(1)}, u32[]{:S(2)}, u32[]{:S(2)}) collective-permute-start(s32[16]{0:T(128)S(1)} %get-tuple-element.9), channel_id=1, source_target_pairs={{0,8},{4,12},{8,16},{12,20},{16,24},{20,28},{24,0},{28,4},{1,9},{5... | collective-permute-start | bytes 200 | tf_op jit(solution)/shard_map/ppermute | solution.py:10
  4.5 10.4 %collective-permute-start.1 = (s32[16]{0:T(128)S(1)}, s32[16]{0:T(128)S(1)}, u32[]{:S(2)}, u32[]{:S(2)}) collective-permute-start(s32[16]{0:T(128)S(1)} %get-tuple-element.8), channel_id=1, source_target_pairs={{0,8},{4,12},{8,16},{12,20},{16,24},{20,28},{24,0},{28,4},{1,9},{5... | collective-permute-start | bytes 200 | tf_op jit(solution)/shard_map/ppermute | solution.py:10
  25.0 9.4 %all-to-all-start.1 = ((bf16[4,4,8192]{2,1,0:T(4,128)(2,1)}), bf16[4,4,8192]{2,1,0:T(4,128)(2,1)S(1)}, u32[]{:S(2)}, u32[]{:S(2)}) async-start(bf16[4,4,8192]{2,1,0:T(4,128)(2,1)} %broadcast_select_fusion), calls=%async_computation.1 | async-start | bytes 524288 | tf_op jit(solution)/shard_map/all_to_all | solution.py:49
  35.2 7.9 %collective-permute-start.2 = (bf16[16,8192]{1,0:T(8,128)(2,1)S(1)}, bf16[16,8192]{1,0:T(8,128)(2,1)S(1)}, u32[]{:S(2)}, u32[]{:S(2)}) collective-permute-start(bf16[16,8192]{1,0:T(8,128)(2,1)S(1)} %gather_fusion.1), channel_id=1, source_target_pairs={{0,24},{4,28},{8,0},{12,4},{16,8},{20,12},{24,16},{28,20},{1,25},{... | collective-permute-start | bytes 786440 | tf_op jit(solution)/shard_map/ppermute | solution.py:10
  37.5 5.6 %copy-start.1 = (bf16[16,8192]{1,0:T(8,128)(2,1)S(1)}, bf16[16,8192]{1,0:T(8,128)(2,1)}, u32[]{:S(2)}) copy-start(bf16[16,8192]{1,0:T(8,128)(2,1)} %param.6) | copy-start | bytes 786436
where the time goes:
time: 85.1 us; the launch traced here: 84.6 us
  blocking collectives  51.3 us (60%)
  starting transfers between devices  10.4 us (12%)
  other arithmetic  9.7 us (11%)
  waiting for transfers between devices  8.44 us (10%)
  local copies, waits for them, and re-layouts  4.12 us (5%)
    psum x1, blocking collectives, shards(): total = lax.psum(terms, ('grp', 'fsdp'))  39.6 us
    ppermute x3, starting transfers between devices, shifted(): return lax.ppermute(value, axis, pairs)  6.95 us
    all_to_all x1, blocking collectives, shards(): lax.all_to_all(places.reshape(groups, capacity), 'fsdp', split_axis=0, co...  6.33 us
    all_to_all x1, waiting for transfers between devices, shards(): lax.all_to_all(asked, 'fsdp', split_axis=0, concat_axis=0, tiled=True)  5.35 us
    all_gather x1, blocking collectives, shards(): lax.all_gather(gain, 'fsdp', axis=0, tiled=True).astype(jnp.float32)  5.3 us
    all_to_all x1, starting transfers between devices, shards(): lax.all_to_all(asked, 'fsdp', split_axis=0, concat_axis=0, tiled=True)  3.41 us
    ppermute x3, waiting for transfers between devices, shifted(): return lax.ppermute(value, axis, pairs)  3.09 us
    reduce_sum x1, other arithmetic, shards(): text_terms = jnp.sum(upper * values * inv * (1.0 - marks)[:, None], axis=0)  2.52 us
  transfers between devices with their start and end apart: 4, of which 2 were waited for; matrix products, arithmetic and copies ran while one was open for 8% of the time, Pallas kernels for 0%

commit v1 on v0

v1 whole, which is shorter than its diff:
```python
import functools

import jax
import jax.numpy as jnp
from jax import lax
from jax.experimental import pallas as pl
from jax.experimental.pallas import tpu as pltpu
from jax.sharding import PartitionSpec as P

MESH = pl.DeviceIdType.MESH
F32 = jnp.float32
LANES = 128
PIECES = 4


def one_where(condition):
    return jnp.where(condition, 1.0, 0.0).astype(F32)


def iota(shape, dim):
    return lax.broadcasted_iota(jnp.int32, shape, dim).astype(F32)


def as_column(row):
    n = row.shape[1]
    diagonal = iota((n, n), 0) == iota((n, n), 1)
    return jnp.sum(jnp.where(diagonal, jnp.broadcast_to(row, (n, n)), 0.0), axis=1, keepdims=True)


def fold(value):
    total = value[0:8]
    for at in range(8, value.shape[0], 8):
        total = total + value[at : at + 8]
    return total


def kernel(
    n_grp, n_fsdp, hop, capacity,
    token_ref, gain_ref, vision_ref, text_hbm, cot_hbm,
    grad_ref, share_ref,
    text, cot, token_out, tokens, gains, rows_out, rows_in, own, terms, first_out, first_in, second,
    load_sem, token_send, token_recv, gain_send, gain_recv, rows_send, rows_recv,
    first_send, first_recv, second_send, second_recv,
):
    g, f = lax.axis_index("grp"), lax.axis_index("fsdp")
    tok_dev, width = text.shape
    vis_dev = vision_ref.shape[0]
    share = width // n_fsdp
    piece = share // PIECES
    block = capacity * n_fsdp
    ahead, behind = lax.rem(g + hop, n_grp), lax.rem(g + n_grp - hop, n_grp)

    load_cot = pltpu.make_async_copy(cot_hbm, cot, load_sem.at[0])
    load_text = pltpu.make_async_copy(text_hbm, text, load_sem.at[1])
    load_text.start()
    load_cot.start()

    barrier = pltpu.get_barrier_semaphore()
    for s in range(n_fsdp):
        pl.semaphore_signal(barrier, inc=1, device_id=(ahead, s), device_id_type=MESH)
        pl.semaphore_signal(barrier, inc=1, device_id=(behind, s), device_id_type=MESH)
    for d in range(1, n_fsdp):
        pl.semaphore_signal(barrier, inc=1, device_id=(g, lax.rem(f + d, n_fsdp)), device_id_type=MESH)

    def greet(d, carry):
        pl.semaphore_signal(barrier, inc=1, device_id=(lax.rem(g + d, n_grp), f), device_id_type=MESH)
        return carry

    lax.fori_loop(1, n_grp, greet, 0)
    token_out[...] = jnp.zeros_like(token_out)
    token_out[:, 0:vis_dev] = token_ref[...]
    gains[f] = gain_ref[...].astype(F32)
    pl.semaphore_wait(barrier, 3 * n_fsdp + n_grp - 2)

    token_copies = []
    for s in range(n_fsdp):
        copy = pltpu.make_async_remote_copy(
            token_out, tokens.at[f], token_send.at[s], token_recv.at[f],
            device_id=(ahead, s), device_id_type=MESH,
        )
        copy.start()
        token_copies.append(copy)
    gain_copies = []
    for d in range(1, n_fsdp):
        copy = pltpu.make_async_remote_copy(
            gains.at[f], gains.at[f], gain_send.at[d - 1], gain_recv.at[d - 1],
            device_id=(g, lax.rem(f + d, n_fsdp)), device_id_type=MESH,
        )
        copy.start()
        gain_copies.append(copy)

    load_text.wait()

    def squares(c, total):
        value = text[:, pl.ds(pl.multiple_of(c * LANES, LANES), LANES)].astype(F32)
        return total + value * value

    total = lax.fori_loop(0, width // LANES, squares, jnp.zeros((tok_dev, LANES), F32), unroll=4)
    inv = lax.rsqrt(jnp.sum(total, axis=1, keepdims=True) / width + 1e-06)
    total = jnp.zeros((vis_dev, LANES), F32)
    for c in range(0, width, LANES):
        value = vision_ref[:, c : c + LANES].astype(F32)
        total = total + value * value
    inv_vision = lax.rsqrt(jnp.sum(total, axis=1, keepdims=True) / width + 1e-06)

    mine = token_ref[...].astype(F32)
    mine_column = as_column(mine)
    start = (ahead * (n_fsdp * tok_dev)).astype(F32)
    target_row, target_column = jnp.zeros_like(mine), jnp.zeros_like(mine_column)
    for t in range(1, n_fsdp):
        target_row += one_where(mine >= start + float(t * tok_dev))
        target_column += one_where(mine_column >= start + float(t * tok_dev))
    square = (vis_dev, vis_dev)
    same = one_where((target_row == target_column) & (iota(square, 1) < iota(square, 0)))
    rank_column = jnp.sum(same, axis=1, keepdims=True)
    wide = (vis_dev, n_fsdp * block)
    places = []
    for q in range(n_fsdp):
        slot = target_column * block + (q * capacity) + rank_column
        places.append(one_where(iota(wide, 1) == slot).astype(jnp.bfloat16))

    base = ((g * n_fsdp + f) * tok_dev).astype(F32)
    marks = jnp.zeros((tok_dev, vis_dev), F32)
    asked = []
    for s in range(n_fsdp):
        pltpu.make_async_remote_copy(
            token_out, tokens.at[s], token_send.at[s], token_recv.at[s],
            device_id=(behind, s), device_id_type=MESH,
        ).wait_recv()
        row = tokens[s][:, 0:vis_dev].astype(F32) - base
        column = as_column(row)
        marks += one_where(iota((tok_dev, vis_dev), 0) == row)
        here_row = (row >= 0.0) & (row < float(tok_dev))
        here_column = one_where((column >= 0.0) & (column < float(tok_dev)))
        rank_row = jnp.sum(
            jnp.where(iota(square, 0) < iota(square, 1), jnp.broadcast_to(here_column, square), 0.0),
            axis=0, keepdims=True,
        )
        rank_row = jnp.where(here_row, rank_row, -1.0)
        hit = one_where(iota((vis_dev, tok_dev), 1) == column)
        line = lax.broadcasted_iota(jnp.int32, (block, vis_dev), 0)
        pick = one_where(lax.rem(line, capacity).astype(F32) == rank_row)
        asked.append(
            jnp.dot(pick.astype(jnp.bfloat16), hit.astype(jnp.bfloat16), preferred_element_type=F32)
        )
    asked = jnp.concatenate(asked, axis=0)
    line = lax.rem(lax.broadcasted_iota(jnp.int32, asked.shape, 0), block)
    picks = [
        jnp.where((line >= q * capacity) & (line < (q + 1) * capacity), asked, 0.0).astype(jnp.bfloat16)
        for q in range(n_fsdp)
    ]

    load_cot.wait()
    row_copies = []
    for k in range(PIECES):
        picked = jnp.zeros((n_fsdp * block, piece), F32)
        for q in range(n_fsdp):
            at = q * share + k * piece
            picked += jnp.dot(picks[q], cot[:, at : at + piece], preferred_element_type=F32)
        rows_out[:, :, k * piece : (k + 1) * piece] = picked.astype(jnp.bfloat16).reshape(n_fsdp, block, piece)
        for s in range(n_fsdp):
            copy = pltpu.make_async_remote_copy(
                rows_out.at[s, :, k * piece : (k + 1) * piece],
                rows_in.at[f, :, k * piece : (k + 1) * piece],
                rows_send.at[k, s], rows_recv.at[k, f],
                device_id=(behind, s), device_id_type=MESH,
            )
            copy.start()
            row_copies.append(copy)

    weight = jnp.broadcast_to(inv * (1.0 - jnp.sum(marks, axis=1, keepdims=True)), (tok_dev, LANES))

    def text_terms(c, carry):
        at = pl.ds(pl.multiple_of(c * LANES, LANES), LANES)
        terms[:, at] = fold(cot[:, at].astype(F32) * text[:, at].astype(F32) * weight)
        return carry

    lax.fori_loop(0, width // LANES, text_terms, 0, unroll=2)

    for copy in gain_copies:
        copy.wait_send()
    for d in range(1, n_fsdp):
        source = lax.rem(f + n_fsdp - d, n_fsdp)
        pltpu.make_async_remote_copy(
            gains.at[f], gains.at[source], gain_send.at[d - 1], gain_recv.at[d - 1],
            device_id=(g, source), device_id_type=MESH,
        ).wait_recv()

    inner = jnp.zeros((vis_dev, 1), F32)
    for k in range(PIECES):
        cut = slice(k * piece, (k + 1) * piece)
        for s in range(n_fsdp):
            pltpu.make_async_remote_copy(
                rows_out.at[s, :, cut], rows_in.at[s, :, cut],
                rows_send.at[k, s], rows_recv.at[k, s],
                device_id=(ahead, s), device_id_type=MESH,
            ).wait_recv()
        arrived = rows_in[:, :, cut].reshape(n_fsdp * block, piece)
        for q in range(n_fsdp):
            at = q * share + k * piece
            upper = jnp.dot(places[q], arrived, preferred_element_type=F32)
            value = vision_ref[:, at : at + piece].astype(F32)
            product = upper * value
            terms[:, at : at + piece] += fold(product * inv_vision)
            inner += jnp.sum(product * gains[q, :, cut], axis=1, keepdims=True)
            own[:, at : at + piece] = upper

    for q in range(n_fsdp):
        first_out[q] = jnp.sum(terms[:, q * share : (q + 1) * share], axis=0, keepdims=True)
    first_copies = []
    for d in range(1, n_fsdp):
        peer = lax.rem(f + d, n_fsdp)
        copy = pltpu.make_async_remote_copy(
            first_out.at[peer], first_in.at[d - 1], first_send.at[d - 1], first_recv.at[d - 1],
            device_id=(g, peer), device_id_type=MESH,
        )
        copy.start()
        first_copies.append(copy)

    factor = inv_vision * inv_vision * inv_vision * (inner / width)
    for q in range(n_fsdp):
        for k in range(PIECES):
            at = q * share + k * piece
            scaled = own[:, at : at + piece] * gains[q, :, k * piece : (k + 1) * piece]
            value = vision_ref[:, at : at + piece].astype(F32)
            grad_ref[:, at : at + piece] = (inv_vision * scaled - value * factor).astype(jnp.bfloat16)

    part = first_out[f]
    for d in range(1, n_fsdp):
        first_copies[d - 1].wait_recv()
        part = part + first_in[d - 1]
    second[g] = part

    def send(d, carry):
        peer = lax.rem(g + d, n_grp)
        pltpu.make_async_remote_copy(
            second.at[g], second.at[g], second_send.at[peer], second_recv.at[g],
            device_id=(peer, f), device_id_type=MESH,
        ).start()
        return carry

    def arrive(d, carry):
        peer = lax.rem(g + d, n_grp)
        copy = pltpu.make_async_remote_copy(
            second.at[peer], second.at[peer], second_send.at[peer], second_recv.at[peer],
            device_id=(peer, f), device_id_type=MESH,
        )
        copy.wait_recv()
        copy.wait_send()
        return carry

    lax.fori_loop(1, n_grp, send, 0)
    for copy in token_copies + row_copies + first_copies:
        copy.wait_send()
    lax.fori_loop(1, n_grp, arrive, 0)
    whole = second[0]
    for at in range(1, n_grp):
        whole = whole + second[at]
    share_ref[...] = whole


def shards(n_grp, n_fsdp, text, vision, vision_token, gain, cotangent):
    hop = n_grp // 4
    tok_dev, width = text.shape
    vis_dev = vision.shape[0]
    capacity = vis_dev // 4
    share = width // n_fsdp
    block = capacity * n_fsdp
    bf16 = jnp.bfloat16
    vmem, dma = pltpu.VMEM, pltpu.SemaphoreType.DMA
    inside = pl.BlockSpec(memory_space=pltpu.VMEM)
    outside = pl.BlockSpec(memory_space=pl.ANY)
    vision_grad, gain_grad = pl.pallas_call(
        functools.partial(kernel, n_grp, n_fsdp, hop, capacity),
        out_shape=(
            jax.ShapeDtypeStruct((vis_dev, width), bf16),
            jax.ShapeDtypeStruct((1, share), F32),
        ),
        in_specs=[inside, inside, inside, outside, outside],
        out_specs=(inside, inside),
        scratch_shapes=[
            vmem((tok_dev, width), bf16),
            vmem((tok_dev, width), bf16),
            vmem((1, LANES), jnp.int32),
            vmem((n_fsdp, 1, LANES), jnp.int32),
            vmem((n_fsdp, 1, share), F32),
            vmem((n_fsdp, block, share), bf16),
            vmem((n_fsdp, block, share), bf16),
            vmem((vis_dev, width), F32),
            vmem((8, width), F32),
            vmem((n_fsdp, 1, share), F32),
            vmem((n_fsdp - 1, 1, share), F32),
            vmem((n_grp, 1, share), F32),
            dma((2,)),
            dma((n_fsdp,)),
            dma((n_fsdp,)),
            dma((n_fsdp - 1,)),
            dma((n_fsdp - 1,)),
            dma((PIECES, n_fsdp)),
            dma((PIECES, n_fsdp)),
            dma((n_fsdp - 1,)),
            dma((n_fsdp - 1,)),
            dma((n_grp,)),
            dma((n_grp,)),
        ],
        compiler_params=pltpu.CompilerParams(
            collective_id=0, has_side_effects=True, vmem_limit_bytes=32 * 1024 * 1024
        ),
    )(vision_token.reshape(1, vis_dev), gain.reshape(1, share), vision, text, cotangent)
    return (vision_grad, gain_grad.reshape(share))


def solution(mesh):
    return jax.shard_map(
        functools.partial(shards, mesh.shape["grp"], mesh.shape["fsdp"]),
        mesh=mesh,
        in_specs=(
            P(("grp", "fsdp"), None),
            P(("grp", "fsdp"), None),
            P(("grp", "fsdp")),
            P("fsdp"),
            P(("grp", "fsdp"), None),
        ),
        out_specs=(P(("grp", "fsdp"), None), P("fsdp")),
        check_vma=False,
    )
```

time: 85.1 us -> 33.6 us (0.39)
  blocking collectives: 51.3 us -> 0 us
  Pallas kernels: 0 us -> 25.9 us
  starting transfers between devices: 10.4 us -> 0 us
  other arithmetic: 9.7 us -> 0 us
  waiting for transfers between devices: 8.44 us -> 0 us
  local copies, waits for them, and re-layouts: 4.12 us -> 6.78 us
    psum x1 -> x0, blocking collectives: 39.6 us -> none  [shards(): total = lax.psum(terms, ('grp', 'fsdp'))]
    pallas_call x0 -> x1, Pallas kernels: none -> 25.9 us  [shards(): pl.pallas_call(functools.partial(kernel, n_grp, n_fsdp, hop, capacity), o...]
    ppermute x3 -> x0, starting transfers between devices: 6.95 us -> none  [shifted(): return lax.ppermute(value, axis, pairs)]
    all_to_all x1 -> x0, blocking collectives: 6.33 us -> none  [shards(): lax.all_to_all(places.reshape(groups, capacity), 'fsdp', split_axis=0, co...]
    reduce_sum x5 -> x0, other arithmetic: 6.24 us -> none  [the longest x1 2.52 us: shards(): text_terms = jnp.sum(upper * values * inv * (1.0 - marks)[:, None], axis=0)]
    unnamed x4 -> x10, local copies, waits for them, and re-layouts: 0.01 us -> 6.09 us
    all_to_all x1 -> x0, waiting for transfers between devices: 5.35 us -> none  [shards(): lax.all_to_all(asked, 'fsdp', split_axis=0, concat_axis=0, tiled=True)]
    all_gather x1 -> x0, blocking collectives: 5.3 us -> none  [shards(): lax.all_gather(gain, 'fsdp', axis=0, tiled=True).astype(jnp.float32)]
  transfers between devices with their start and end apart: 4 -> 0, of which waited for: 2 -> 0; matrix products, arithmetic and copies ran while one was open for 8% -> 0% of each run, Pallas kernels for 0% -> 0%
where the time goes in v1:
time: 33.6 us; the launch traced here: 33.4 us
  Pallas kernels  25.9 us (77%)
  local copies, waits for them, and re-layouts  6.78 us (20%)
  between operations  0.64 us (2%)
    pallas_call x1, Pallas kernels, shards(): pl.pallas_call(functools.partial(kernel, n_grp, n_fsdp, hop, capacity), o...  25.9 us
    unnamed x10, local copies, waits for them, and re-layouts  6.09 us
    reshape x1, local copies, waits for them, and re-layouts, shards(): gain.reshape(1, share)  0.69 us

profile of v1, /device:TPU:0, one launch (start us, length us, event | category | flops | bytes accessed | tf_op | source)
XLA Modules:
  0.0 33.4 jit_solution(16491603000657551967)
XLA Ops:
  0.6 0.7 %reshape.14.gain_ref = bf16[1,2048]{1,0:T(2,128)(2,1)S(1)} reshape(bf16[2048]{0:T(1024)(128)(2,1)} %param.8) | data formatting | bytes 8192 | tf_op jit(solution)/shard_map/reshape | solution.py:309
  1.3 0.0 copy-start
  1.3 1.6 %copy-done = bf16[128,8192]{1,0:T(8,128)(2,1)S(1)} copy-done((bf16[128,8192]{1,0:T(8,128)(2,1)S(1)}, bf16[128,8192]{1,0:T(8,128)(2,1)}, u32[]{:S(2)}) %copy-start) | copy-done | bytes 2097176
  2.9 0.0 copy-start.1
  2.9 1.6 %copy-done.1 = bf16[128,8192]{1,0:T(8,128)(2,1)S(1)} copy-done((bf16[128,8192]{1,0:T(8,128)(2,1)S(1)}, bf16[128,8192]{1,0:T(8,128)(2,1)}, u32[]{:S(2)}) %copy-start.1) | copy-done | bytes 2097176
  4.5 0.0 copy-start.2
  4.5 0.9 %copy-done.2 = bf16[16,8192]{1,0:T(8,128)(2,1)S(1)} copy-done((bf16[16,8192]{1,0:T(8,128)(2,1)S(1)}, bf16[16,8192]{1,0:T(8,128)(2,1)}, u32[]{:S(2)}) %copy-start.2) | copy-done | bytes 262168
  5.5 0.0 copy-start.3
  5.5 0.7 %copy-done.3 = s32[16]{0:T(128)S(1)} copy-done((s32[16]{0:T(128)S(1)}, s32[16]{0:T(128)}, u32[]{:S(2)}) %copy-start.3) | copy-done | bytes 88
  6.1 25.9 %shard_map.68 = (bf16[16,8192]{1,0:T(8,128)(2,1)S(1)}, f32[1,2048]{1,0:T(1,128)S(1)}) custom-call(s32[1,16]{1,0:T(1,128)S(1)} %bitcast.3, bf16[1,2048]{1,0:T(2,128)(2,1)S(1)} %reshape.14.gain_ref, bf16[16,8192]{1,0:T(8,128)(2,1)S(1)} %copy-done.2, bf16[128,8192]{1,0:T(8,128)(2,1)S(1)} %copy-done, bf16[128,8192]{1,0:T(8,128)(2,1)S(1)} %copy-done.1), custom_call_target="tpu_custom_call" | custom-call | tf_op jit(solution)/shard_map/pallas_call | solution.py:273
  32.1 0.7 %copy.9 = bf16[16,8192]{1,0:T(8,128)(2,1)} copy(bf16[16,8192]{1,0:T(8,128)(2,1)S(1)} %get-tuple-element.8) | data formatting | bytes 524288
  32.8 0.6 %copy.10 = f32[2048]{0:T(1024)} copy(f32[2048]{0:T(1024)S(1)} %bitcast.2) | data formatting | bytes 16384
Async XLA Ops:
  1.3 1.6 %copy-start = (bf16[128,8192]{1,0:T(8,128)(2,1)S(1)}, bf16[128,8192]{1,0:T(8,128)(2,1)}, u32[]{:S(2)}) copy-start(bf16[128,8192]{1,0:T(8,128)(2,1)} %text_hbm.1) | copy-start | bytes 6291460
  2.9 1.6 %copy-start.1 = (bf16[128,8192]{1,0:T(8,128)(2,1)S(1)}, bf16[128,8192]{1,0:T(8,128)(2,1)}, u32[]{:S(2)}) copy-start(bf16[128,8192]{1,0:T(8,128)(2,1)} %cot_hbm.1) | copy-start | bytes 6291460
  4.5 0.9 %copy-start.2 = (bf16[16,8192]{1,0:T(8,128)(2,1)S(1)}, bf16[16,8192]{1,0:T(8,128)(2,1)}, u32[]{:S(2)}) copy-start(bf16[16,8192]{1,0:T(8,128)(2,1)} %vision_ref.1) | copy-start | bytes 786436
  5.5 0.7 %copy-start.3 = (s32[16]{0:T(128)S(1)}, s32[16]{0:T(128)}, u32[]{:S(2)}) copy-start(s32[16]{0:T(128)} %param.7) | copy-start | bytes 196

commit v2 on v1

--- a/solution.py
+++ b/solution.py
@@ -36,10 +36,11 @@
 
 def kernel(
     n_grp, n_fsdp, hop, capacity,
-    token_ref, gain_ref, vision_ref, text_hbm, cot_hbm,
+    token_hbm, gain_hbm, vision_hbm, text_hbm, cot_hbm,
     grad_ref, share_ref,
-    text, cot, token_out, tokens, gains, rows_out, rows_in, own, terms, first_out, first_in, second,
-    load_sem, token_send, token_recv, gain_send, gain_recv, rows_send, rows_recv,
+    text, cot, vision_ref, token_ref, slots_out, slots_in, gains, rows_out, rows_in, own, terms,
+    first_out, first_in, second,
+    load_sem, slot_send, slot_recv, gain_send, gain_recv, rows_send, rows_recv,
     first_send, first_recv, second_send, second_recv,
 ):
     g, f = lax.axis_index("grp"), lax.axis_index("fsdp")
@@ -48,12 +49,15 @@
     share = width // n_fsdp
     piece = share // PIECES
     block = capacity * n_fsdp
+    lines = slots_out.shape[1]
     ahead, behind = lax.rem(g + hop, n_grp), lax.rem(g + n_grp - hop, n_grp)
 
-    load_cot = pltpu.make_async_copy(cot_hbm, cot, load_sem.at[0])
-    load_text = pltpu.make_async_copy(text_hbm, text, load_sem.at[1])
-    load_text.start()
-    load_cot.start()
+    load_token = pltpu.make_async_copy(token_hbm, token_ref, load_sem.at[0])
+    load_gain = pltpu.make_async_copy(gain_hbm, gains.at[f], load_sem.at[1])
+    load_cot = pltpu.make_async_copy(cot_hbm, cot, load_sem.at[2])
+    load_vision = pltpu.make_async_copy(vision_hbm, vision_ref, load_sem.at[3])
+    load_text = pltpu.make_async_copy(text_hbm, text, load_sem.at[4])
+    load_token.start()
 
     barrier = pltpu.get_barrier_semaphore()
     for s in range(n_fsdp):
@@ -67,19 +71,43 @@
         return carry
 
     lax.fori_loop(1, n_grp, greet, 0)
-    token_out[...] = jnp.zeros_like(token_out)
-    token_out[:, 0:vis_dev] = token_ref[...]
-    gains[f] = gain_ref[...].astype(F32)
+    load_gain.start()
+    load_cot.start()
+    load_vision.start()
+    load_text.start()
+
+    load_token.wait()
+    mine = token_ref[...].astype(F32) - (ahead * (n_fsdp * tok_dev)).astype(F32)
+    mine_column = as_column(mine)
+    target_row, target_column = jnp.zeros_like(mine), jnp.zeros_like(mine_column)
+    for t in range(1, n_fsdp):
+        target_row += one_where(mine >= float(t * tok_dev))
+        target_column += one_where(mine_column >= float(t * tok_dev))
+    square = (vis_dev, vis_dev)
+    same = target_row == target_column
+    rank_column = jnp.sum(
+        one_where(same & (iota(square, 1) < iota(square, 0))), axis=1, keepdims=True
+    )
+    rank_row = jnp.sum(
+        one_where(same & (iota(square, 0) < iota(square, 1))), axis=0, keepdims=True
+    )
+    local = mine - target_row * float(tok_dev)
+    line = lax.rem(lax.broadcasted_iota(jnp.int32, (lines, vis_dev), 0), capacity).astype(F32)
+    for t in range(n_fsdp):
+        chosen = (line == rank_row) & (target_row == float(t))
+        number = jnp.sum(jnp.where(chosen, local + 1.0, 0.0), axis=1, keepdims=True) - 1.0
+        slots_out[t] = jnp.broadcast_to(number, (lines, LANES))
     pl.semaphore_wait(barrier, 3 * n_fsdp + n_grp - 2)
 
-    token_copies = []
+    slot_copies = []
     for s in range(n_fsdp):
         copy = pltpu.make_async_remote_copy(
-            token_out, tokens.at[f], token_send.at[s], token_recv.at[f],
+            slots_out.at[s], slots_in.at[f], slot_send.at[s], slot_recv.at[f],
             device_id=(ahead, s), device_id_type=MESH,
         )
         copy.start()
-        token_copies.append(copy)
+        slot_copies.append(copy)
+    load_gain.wait()
     gain_copies = []
     for d in range(1, n_fsdp):
         copy = pltpu.make_async_remote_copy(
@@ -89,68 +117,33 @@
         copy.start()
         gain_copies.append(copy)
 
-    load_text.wait()
-
-    def squares(c, total):
-        value = text[:, pl.ds(pl.multiple_of(c * LANES, LANES), LANES)].astype(F32)
-        return total + value * value
-
-    total = lax.fori_loop(0, width // LANES, squares, jnp.zeros((tok_dev, LANES), F32), unroll=4)
-    inv = lax.rsqrt(jnp.sum(total, axis=1, keepdims=True) / width + 1e-06)
+    wide = (vis_dev, n_fsdp * block)
+    places = []
+    for q in range(n_fsdp):
+        slot = target_column * block + (q * capacity) + rank_column
+        places.append(one_where(iota(wide, 1) == slot).astype(jnp.bfloat16))
+    load_vision.wait()
     total = jnp.zeros((vis_dev, LANES), F32)
     for c in range(0, width, LANES):
         value = vision_ref[:, c : c + LANES].astype(F32)
         total = total + value * value
     inv_vision = lax.rsqrt(jnp.sum(total, axis=1, keepdims=True) / width + 1e-06)
-
-    mine = token_ref[...].astype(F32)
-    mine_column = as_column(mine)
-    start = (ahead * (n_fsdp * tok_dev)).astype(F32)
-    target_row, target_column = jnp.zeros_like(mine), jnp.zeros_like(mine_column)
-    for t in range(1, n_fsdp):
-        target_row += one_where(mine >= start + float(t * tok_dev))
-        target_column += one_where(mine_column >= start + float(t * tok_dev))
-    square = (vis_dev, vis_dev)
-    same = one_where((target_row == target_column) & (iota(square, 1) < iota(square, 0)))
-    rank_column = jnp.sum(same, axis=1, keepdims=True)
-    wide = (vis_dev, n_fsdp * block)
-    places = []
-    for q in range(n_fsdp):
-        slot = target_column * block + (q * capacity) + rank_column
-        places.append(one_where(iota(wide, 1) == slot).astype(jnp.bfloat16))
-
-    base = ((g * n_fsdp + f) * tok_dev).astype(F32)
-    marks = jnp.zeros((tok_dev, vis_dev), F32)
+    load_cot.wait()
+
     asked = []
     for s in range(n_fsdp):
         pltpu.make_async_remote_copy(
-            token_out, tokens.at[s], token_send.at[s], token_recv.at[s],
+            slots_out.at[s], slots_in.at[s], slot_send.at[s], slot_recv.at[s],
             device_id=(behind, s), device_id_type=MESH,
         ).wait_recv()
-        row = tokens[s][:, 0:vis_dev].astype(F32) - base
-        column = as_column(row)
-        marks += one_where(iota((tok_dev, vis_dev), 0) == row)
-        here_row = (row >= 0.0) & (row < float(tok_dev))
-        here_column = one_where((column >= 0.0) & (column < float(tok_dev)))
-        rank_row = jnp.sum(
-            jnp.where(iota(square, 0) < iota(square, 1), jnp.broadcast_to(here_column, square), 0.0),
-            axis=0, keepdims=True,
-        )
-        rank_row = jnp.where(here_row, rank_row, -1.0)
-        hit = one_where(iota((vis_dev, tok_dev), 1) == column)
-        line = lax.broadcasted_iota(jnp.int32, (block, vis_dev), 0)
-        pick = one_where(lax.rem(line, capacity).astype(F32) == rank_row)
-        asked.append(
-            jnp.dot(pick.astype(jnp.bfloat16), hit.astype(jnp.bfloat16), preferred_element_type=F32)
-        )
+        number = slots_in[s][:, 0:tok_dev] if tok_dev <= LANES else pltpu.repeat(slots_in[s], tok_dev // LANES, 1)
+        asked += [one_where(iota((lines, tok_dev), 1) == number)] * (block // lines)
     asked = jnp.concatenate(asked, axis=0)
     line = lax.rem(lax.broadcasted_iota(jnp.int32, asked.shape, 0), block)
     picks = [
         jnp.where((line >= q * capacity) & (line < (q + 1) * capacity), asked, 0.0).astype(jnp.bfloat16)
         for q in range(n_fsdp)
     ]
-
-    load_cot.wait()
     row_copies = []
     for k in range(PIECES):
         picked = jnp.zeros((n_fsdp * block, piece), F32)
@@ -168,7 +161,16 @@
             copy.start()
             row_copies.append(copy)
 
-    weight = jnp.broadcast_to(inv * (1.0 - jnp.sum(marks, axis=1, keepdims=True)), (tok_dev, LANES))
+    load_text.wait()
+
+    def squares(c, total):
+        value = text[:, pl.ds(pl.multiple_of(c * LANES, LANES), LANES)].astype(F32)
+        return total + value * value
+
+    total = lax.fori_loop(0, width // LANES, squares, jnp.zeros((tok_dev, LANES), F32), unroll=4)
+    inv = lax.rsqrt(jnp.sum(total, axis=1, keepdims=True) / width + 1e-06)
+    marks = as_column(jnp.sum(jnp.where(line < capacity, asked, 0.0), axis=0, keepdims=True))
+    weight = jnp.broadcast_to(inv * (1.0 - marks), (tok_dev, LANES))
 
     def text_terms(c, carry):
         at = pl.ds(pl.multiple_of(c * LANES, LANES), LANES)
@@ -186,7 +188,13 @@
             device_id=(g, source), device_id_type=MESH,
         ).wait_recv()
 
-    inner = jnp.zeros((vis_dev, 1), F32)
+    gain_rows = []
+    for q in range(n_fsdp):
+        tiles = gains[q].astype(F32)
+        flat = jnp.concatenate([tiles[c : c + 1] for c in range(tiles.shape[0])], axis=1)
+        gain_rows.append([flat[:, k * piece : (k + 1) * piece] for k in range(PIECES)])
+
+    inner = jnp.zeros((vis_dev, LANES), F32)
     for k in range(PIECES):
         cut = slice(k * piece, (k + 1) * piece)
         for s in range(n_fsdp):
@@ -202,7 +210,9 @@
             value = vision_ref[:, at : at + piece].astype(F32)
             product = upper * value
             terms[:, at : at + piece] += fold(product * inv_vision)
-            inner += jnp.sum(product * gains[q, :, cut], axis=1, keepdims=True)
+            product = product * gain_rows[q][k]
+            for c in range(0, piece, LANES):
+                inner += product[:, c : c + LANES]
             own[:, at : at + piece] = upper
 
     for q in range(n_fsdp):
@@ -217,11 +227,12 @@
         copy.start()
         first_copies.append(copy)
 
-    factor = inv_vision * inv_vision * inv_vision * (inner / width)
+    inner = jnp.sum(inner, axis=1, keepdims=True) / width
+    factor = inv_vision * inv_vision * inv_vision * inner
     for q in range(n_fsdp):
         for k in range(PIECES):
             at = q * share + k * piece
-            scaled = own[:, at : at + piece] * gains[q, :, k * piece : (k + 1) * piece]
+            scaled = own[:, at : at + piece] * gain_rows[q][k]
             value = vision_ref[:, at : at + piece].astype(F32)
             grad_ref[:, at : at + piece] = (inv_vision * scaled - value * factor).astype(jnp.bfloat16)
 
@@ -250,7 +261,7 @@
         return carry
 
     lax.fori_loop(1, n_grp, send, 0)
-    for copy in token_copies + row_copies + first_copies:
+    for copy in slot_copies + row_copies + first_copies:
         copy.wait_send()
     lax.fori_loop(1, n_grp, arrive, 0)
     whole = second[0]
@@ -269,21 +280,23 @@
     bf16 = jnp.bfloat16
     vmem, dma = pltpu.VMEM, pltpu.SemaphoreType.DMA
     inside = pl.BlockSpec(memory_space=pltpu.VMEM)
-    outside = pl.BlockSpec(memory_space=pl.ANY)
+    outside = pl.BlockSpec(memory_space=pltpu.HBM)
     vision_grad, gain_grad = pl.pallas_call(
         functools.partial(kernel, n_grp, n_fsdp, hop, capacity),
         out_shape=(
             jax.ShapeDtypeStruct((vis_dev, width), bf16),
             jax.ShapeDtypeStruct((1, share), F32),
         ),
-        in_specs=[inside, inside, inside, outside, outside],
+        in_specs=[outside] * 5,
         out_specs=(inside, inside),
         scratch_shapes=[
             vmem((tok_dev, width), bf16),
             vmem((tok_dev, width), bf16),
-            vmem((1, LANES), jnp.int32),
-            vmem((n_fsdp, 1, LANES), jnp.int32),
-            vmem((n_fsdp, 1, share), F32),
+            vmem((vis_dev, width), bf16),
+            vmem((1, vis_dev), jnp.int32),
+            vmem((n_fsdp, 2 * capacity, LANES), F32),
+            vmem((n_fsdp, 2 * capacity, LANES), F32),
+            vmem((n_fsdp, share // LANES, LANES), bf16),
             vmem((n_fsdp, block, share), bf16),
             vmem((n_fsdp, block, share), bf16),
             vmem((vis_dev, width), F32),
@@ -291,7 +304,7 @@
             vmem((n_fsdp, 1, share), F32),
             vmem((n_fsdp - 1, 1, share), F32),
             vmem((n_grp, 1, share), F32),
-            dma((2,)),
+            dma((5,)),
             dma((n_fsdp,)),
             dma((n_fsdp,)),
             dma((n_fsdp - 1,)),
@@ -304,9 +317,9 @@
             dma((n_grp,)),
         ],
         compiler_params=pltpu.CompilerParams(
-            collective_id=0, has_side_effects=True, vmem_limit_bytes=32 * 1024 * 1024
+            collective_id=0, has_side_effects=True, vmem_limit_bytes=56 * 1024 * 1024
         ),
-    )(vision_token.reshape(1, vis_dev), gain.reshape(1, share), vision, text, cotangent)
+    )(vision_token.reshape(1, vis_dev), gain.reshape(share // LANES, LANES), vision, text, cotangent)
     return (vision_grad, gain_grad.reshape(share))
 
 

time: 33.6 us -> 29.9 us (0.89)
  local copies, waits for them, and re-layouts: 6.78 us -> 2.96 us
    unnamed x10 -> x2, local copies, waits for them, and re-layouts: 6.09 us -> 2.96 us
    reshape x1 -> x0, local copies, waits for them, and re-layouts: 0.69 us -> none  [shards(): gain.reshape(1, share)]
where the time goes in v2:
time: 29.9 us; the launch traced here: 29.7 us
  Pallas kernels  26.1 us (87%)
  local copies, waits for them, and re-layouts  2.96 us (10%)
  between operations  0.64 us (2%)
    pallas_call x1, Pallas kernels, shards(): pl.pallas_call(functools.partial(kernel, n_grp, n_fsdp, hop, capacity), o...  26.1 us
    unnamed x2, local copies, waits for them, and re-layouts  2.96 us

profile of v2, /device:TPU:0, one launch (start us, length us, event | category | flops | bytes accessed | tf_op | source)
XLA Modules:
  0.0 29.7 jit_solution(5859994651839501633)
XLA Ops:
  0.6 26.1 %shard_map.68 = (bf16[16,8192]{1,0:T(8,128)(2,1)}, f32[1,2048]{1,0:T(1,128)}) custom-call(s32[1,16]{1,0:T(1,128)} %bitcast.5, bf16[16,128]{1,0:T(8,128)(2,1)} %bitcast.4, bf16[16,8192]{1,0:T(8,128)(2,1)} %vision_hbm.1, bf16[128,8192]{1,0:T(8,128)(2,1)} %text_hbm.1, bf16[128,8192]{1,0:T(8,128)(2,1)} %cot_hbm.1), custom_call_target="tpu_custom_call" | custom-call | tf_op jit(solution)/shard_map/pallas_call | solution.py:284
  26.8 1.7 %copy.9 = bf16[16,8192]{1,0:T(8,128)(2,1)} copy(bf16[16,8192]{1,0:T(8,128)(2,1)} %get-tuple-element.8) | data formatting | bytes 524288
  28.4 1.3 %copy.10 = f32[2048]{0:T(1024)} copy(f32[2048]{0:T(1024)} %bitcast.3) | data formatting | bytes 16384

commit v3 on v2

--- a/solution.py
+++ b/solution.py
@@ -281,6 +281,7 @@
     vmem, dma = pltpu.VMEM, pltpu.SemaphoreType.DMA
     inside = pl.BlockSpec(memory_space=pltpu.VMEM)
     outside = pl.BlockSpec(memory_space=pltpu.HBM)
+    hbm = functools.partial(pltpu.with_memory_space_constraint, memory_space=pltpu.HBM)
     vision_grad, gain_grad = pl.pallas_call(
         functools.partial(kernel, n_grp, n_fsdp, hop, capacity),
         out_shape=(
@@ -317,9 +318,12 @@
             dma((n_grp,)),
         ],
         compiler_params=pltpu.CompilerParams(
-            collective_id=0, has_side_effects=True, vmem_limit_bytes=56 * 1024 * 1024
+            collective_id=0, has_side_effects=True, vmem_limit_bytes=32 * 1024 * 1024
         ),
-    )(vision_token.reshape(1, vis_dev), gain.reshape(share // LANES, LANES), vision, text, cotangent)
+    )(
+        hbm(vision_token.reshape(1, vis_dev)), hbm(gain.reshape(share // LANES, LANES)),
+        hbm(vision), hbm(text), hbm(cotangent),
+    )
     return (vision_grad, gain_grad.reshape(share))
 
 

time: 29.9 us -> 27.5 us (0.920)
  local copies, waits for them, and re-layouts: 2.96 us -> 1.3 us
  Pallas kernels: 26.1 us -> 25.4 us
    unnamed x2, local copies, waits for them, and re-layouts: 2.96 us -> 1.3 us
    pallas_call x1, Pallas kernels: 26.1 us -> 25.4 us  [shards(): pl.pallas_call(functools.partial(kernel, n_grp, n_fsdp, hop, capacity), o...]
where the time goes in v3:
time: 27.5 us; the launch traced here: 27.4 us
  Pallas kernels  25.4 us (92%)
  local copies, waits for them, and re-layouts  1.3 us (5%)
  between operations  0.64 us (2%)
    pallas_call x1, Pallas kernels, shards(): pl.pallas_call(functools.partial(kernel, n_grp, n_fsdp, hop, capacity), o...  25.4 us
    unnamed x2, local copies, waits for them, and re-layouts  1.3 us

profile of v3, /device:TPU:0, one launch (start us, length us, event | category | flops | bytes accessed | tf_op | source)
XLA Modules:
  0.0 27.4 jit_solution(14818703964216101646)
XLA Ops:
  0.6 25.4 %shard_map.68 = (bf16[16,8192]{1,0:T(8,128)(2,1)S(1)}, f32[1,2048]{1,0:T(1,128)S(1)}) custom-call(s32[1,16]{1,0:T(1,128)} %bitcast.5, bf16[16,128]{1,0:T(8,128)(2,1)} %bitcast.4, bf16[16,8192]{1,0:T(8,128)(2,1)} %vision_hbm.1, bf16[128,8192]{1,0:T(8,128)(2,1)} %text_hbm.1, bf16[128,8192]{1,0:T(8,128)(2,1)} %cot_hbm.1), custom_call_target="tpu_custom_call" | custom-call | tf_op jit(solution)/shard_map/pallas_call | solution.py:285
  26.1 0.7 %copy.9 = bf16[16,8192]{1,0:T(8,128)(2,1)} copy(bf16[16,8192]{1,0:T(8,128)(2,1)S(1)} %get-tuple-element.8) | data formatting | bytes 524288
  26.8 0.6 %copy.10 = f32[2048]{0:T(1024)} copy(f32[2048]{0:T(1024)S(1)} %bitcast.3) | data formatting | bytes 16384

commit v4 on v3

--- a/solution.py
+++ b/solution.py
@@ -10,7 +10,7 @@
 MESH = pl.DeviceIdType.MESH
 F32 = jnp.float32
 LANES = 128
-PIECES = 4
+PIECES = 1
 
 
 def one_where(condition):
@@ -38,9 +38,10 @@
     n_grp, n_fsdp, hop, capacity,
     token_hbm, gain_hbm, vision_hbm, text_hbm, cot_hbm,
     grad_ref, share_ref,
-    text, cot, vision_ref, token_ref, slots_out, slots_in, gains, rows_out, rows_in, own, terms,
-    first_out, first_in, second,
+    text, cot, vision_ref, token_ref, slots_out, slots_in, gains, rows_out, rows_in, terms, vis_out, vis_in, inv_in,
+    back_out, back_in, share_terms, first_out, first_in, second,
     load_sem, slot_send, slot_recv, gain_send, gain_recv, rows_send, rows_recv,
+    vis_send, vis_recv, inv_send, inv_recv, back_send, back_recv,
     first_send, first_recv, second_send, second_recv,
 ):
     g, f = lax.axis_index("grp"), lax.axis_index("fsdp")
@@ -117,17 +118,6 @@
         copy.start()
         gain_copies.append(copy)
 
-    wide = (vis_dev, n_fsdp * block)
-    places = []
-    for q in range(n_fsdp):
-        slot = target_column * block + (q * capacity) + rank_column
-        places.append(one_where(iota(wide, 1) == slot).astype(jnp.bfloat16))
-    load_vision.wait()
-    total = jnp.zeros((vis_dev, LANES), F32)
-    for c in range(0, width, LANES):
-        value = vision_ref[:, c : c + LANES].astype(F32)
-        total = total + value * value
-    inv_vision = lax.rsqrt(jnp.sum(total, axis=1, keepdims=True) / width + 1e-06)
     load_cot.wait()
 
     asked = []
@@ -137,30 +127,54 @@
             device_id=(behind, s), device_id_type=MESH,
         ).wait_recv()
         number = slots_in[s][:, 0:tok_dev] if tok_dev <= LANES else pltpu.repeat(slots_in[s], tok_dev // LANES, 1)
-        asked += [one_where(iota((lines, tok_dev), 1) == number)] * (block // lines)
+        asked.append(one_where(iota((lines, tok_dev), 1) == number)[0:capacity])
     asked = jnp.concatenate(asked, axis=0)
-    line = lax.rem(lax.broadcasted_iota(jnp.int32, asked.shape, 0), block)
-    picks = [
-        jnp.where((line >= q * capacity) & (line < (q + 1) * capacity), asked, 0.0).astype(jnp.bfloat16)
-        for q in range(n_fsdp)
-    ]
+    picks = asked.astype(jnp.bfloat16)
     row_copies = []
     for k in range(PIECES):
-        picked = jnp.zeros((n_fsdp * block, piece), F32)
-        for q in range(n_fsdp):
-            at = q * share + k * piece
-            picked += jnp.dot(picks[q], cot[:, at : at + piece], preferred_element_type=F32)
-        rows_out[:, :, k * piece : (k + 1) * piece] = picked.astype(jnp.bfloat16).reshape(n_fsdp, block, piece)
+        cut = slice(k * piece, (k + 1) * piece)
+        for s in range(n_fsdp):
+            at = s * share + k * piece
+            picked = jnp.dot(picks, cot[:, at : at + piece], preferred_element_type=F32)
+            rows_out[s, :, cut] = picked.astype(jnp.bfloat16)
         for s in range(n_fsdp):
             copy = pltpu.make_async_remote_copy(
-                rows_out.at[s, :, k * piece : (k + 1) * piece],
-                rows_in.at[f, :, k * piece : (k + 1) * piece],
-                rows_send.at[k, s], rows_recv.at[k, f],
+                rows_out.at[s, :, cut], rows_in.at[f, :, cut], rows_send.at[k, s], rows_recv.at[k, f],
                 device_id=(behind, s), device_id_type=MESH,
             )
             copy.start()
             row_copies.append(copy)
 
+    load_vision.wait()
+    slot_row = target_row * float(capacity) + rank_row
+    slot_column = target_column * float(capacity) + rank_column
+    gather = one_where(iota((block, vis_dev), 0) == slot_row).astype(jnp.bfloat16)
+    scatter = one_where(iota((vis_dev, block), 1) == slot_column).astype(jnp.bfloat16)
+    total = jnp.zeros((block, LANES), F32)
+    for q in range(n_fsdp):
+        for k in range(PIECES):
+            at = q * share + k * piece
+            value = jnp.dot(gather, vision_ref[:, at : at + piece], preferred_element_type=F32)
+            vis_out[q, :, k * piece : (k + 1) * piece] = value.astype(jnp.bfloat16)
+            for c in range(0, piece, LANES):
+                total += value[:, c : c + LANES] * value[:, c : c + LANES]
+    inv_vision = lax.rsqrt(jnp.sum(total, axis=1, keepdims=True) / width + 1e-06)
+    inv_in[f] = jnp.broadcast_to(inv_vision, (block, LANES))
+    vis_in[f] = vis_out[f]
+    vis_copies = []
+    for d in range(1, n_fsdp):
+        peer = lax.rem(f + d, n_fsdp)
+        for source, target, send_sem, recv_sem in (
+            (vis_out.at[peer], vis_in.at[f], vis_send, vis_recv),
+            (inv_in.at[f], inv_in.at[f], inv_send, inv_recv),
+        ):
+            copy = pltpu.make_async_remote_copy(
+                source, target, send_sem.at[d - 1], recv_sem.at[d - 1],
+                device_id=(g, peer), device_id_type=MESH,
+            )
+            copy.start()
+            vis_copies.append(copy)
+
     load_text.wait()
 
     def squares(c, total):
@@ -169,7 +183,7 @@
 
     total = lax.fori_loop(0, width // LANES, squares, jnp.zeros((tok_dev, LANES), F32), unroll=4)
     inv = lax.rsqrt(jnp.sum(total, axis=1, keepdims=True) / width + 1e-06)
-    marks = as_column(jnp.sum(jnp.where(line < capacity, asked, 0.0), axis=0, keepdims=True))
+    marks = as_column(jnp.sum(asked, axis=0, keepdims=True))
     weight = jnp.broadcast_to(inv * (1.0 - marks), (tok_dev, LANES))
 
     def text_terms(c, carry):
@@ -178,42 +192,6 @@
         return carry
 
     lax.fori_loop(0, width // LANES, text_terms, 0, unroll=2)
-
-    for copy in gain_copies:
-        copy.wait_send()
-    for d in range(1, n_fsdp):
-        source = lax.rem(f + n_fsdp - d, n_fsdp)
-        pltpu.make_async_remote_copy(
-            gains.at[f], gains.at[source], gain_send.at[d - 1], gain_recv.at[d - 1],
-            device_id=(g, source), device_id_type=MESH,
-        ).wait_recv()
-
-    gain_rows = []
-    for q in range(n_fsdp):
-        tiles = gains[q].astype(F32)
-        flat = jnp.concatenate([tiles[c : c + 1] for c in range(tiles.shape[0])], axis=1)
-        gain_rows.append([flat[:, k * piece : (k + 1) * piece] for k in range(PIECES)])
-
-    inner = jnp.zeros((vis_dev, LANES), F32)
-    for k in range(PIECES):
-        cut = slice(k * piece, (k + 1) * piece)
-        for s in range(n_fsdp):
-            pltpu.make_async_remote_copy(
-                rows_out.at[s, :, cut], rows_in.at[s, :, cut],
-                rows_send.at[k, s], rows_recv.at[k, s],
-                device_id=(ahead, s), device_id_type=MESH,
-            ).wait_recv()
-        arrived = rows_in[:, :, cut].reshape(n_fsdp * block, piece)
-        for q in range(n_fsdp):
-            at = q * share + k * piece
-            upper = jnp.dot(places[q], arrived, preferred_element_type=F32)
-            value = vision_ref[:, at : at + piece].astype(F32)
-            product = upper * value
-            terms[:, at : at + piece] += fold(product * inv_vision)
-            product = product * gain_rows[q][k]
-            for c in range(0, piece, LANES):
-                inner += product[:, c : c + LANES]
-            own[:, at : at + piece] = upper
 
     for q in range(n_fsdp):
         first_out[q] = jnp.sum(terms[:, q * share : (q + 1) * share], axis=0, keepdims=True)
@@ -227,20 +205,65 @@
         copy.start()
         first_copies.append(copy)
 
-    inner = jnp.sum(inner, axis=1, keepdims=True) / width
-    factor = inv_vision * inv_vision * inv_vision * inner
+    for copy in gain_copies:
+        copy.wait_send()
+    for d in range(1, n_fsdp):
+        source = lax.rem(f + n_fsdp - d, n_fsdp)
+        pltpu.make_async_remote_copy(
+            gains.at[f], gains.at[source], gain_send.at[d - 1], gain_recv.at[d - 1],
+            device_id=(g, source), device_id_type=MESH,
+        ).wait_recv()
+
+    gain_rows = []
     for q in range(n_fsdp):
-        for k in range(PIECES):
-            at = q * share + k * piece
-            scaled = own[:, at : at + piece] * gain_rows[q][k]
-            value = vision_ref[:, at : at + piece].astype(F32)
-            grad_ref[:, at : at + piece] = (inv_vision * scaled - value * factor).astype(jnp.bfloat16)
-
+        tiles = gains[q].astype(F32)
+        flat = jnp.concatenate([tiles[c : c + 1] for c in range(tiles.shape[0])], axis=1)
+        gain_rows.append([flat[:, k * piece : (k + 1) * piece] for k in range(PIECES)])
+
+    for d in range(1, n_fsdp):
+        source = lax.rem(f + n_fsdp - d, n_fsdp)
+        pltpu.make_async_remote_copy(
+            vis_in.at[source], vis_in.at[source], vis_send.at[d - 1], vis_recv.at[d - 1],
+            device_id=(g, source), device_id_type=MESH,
+        ).wait_recv()
+        pltpu.make_async_remote_copy(
+            inv_in.at[source], inv_in.at[source], inv_send.at[d - 1], inv_recv.at[d - 1],
+            device_id=(g, source), device_id_type=MESH,
+        ).wait_recv()
     part = first_out[f]
     for d in range(1, n_fsdp):
         first_copies[d - 1].wait_recv()
         part = part + first_in[d - 1]
-    second[g] = part
+
+    every = n_fsdp * block
+    to = lax.broadcasted_iota(jnp.int32, (every, every), 0)
+    within = lax.rem(to, block)
+    place = lax.rem(within, capacity)
+    origin = (within - place) * n_fsdp + lax.div(to - within, n_fsdp) + place
+    order = one_where(lax.broadcasted_iota(jnp.int32, (every, every), 1) == origin).astype(jnp.bfloat16)
+    inv_all = inv_in[...].reshape(every, LANES)[:, 0:1]
+    back_copies = []
+    for k in range(PIECES):
+        cut = slice(k * piece, (k + 1) * piece)
+        for s in range(n_fsdp):
+            pltpu.make_async_remote_copy(
+                rows_out.at[s, :, cut], rows_in.at[s, :, cut], rows_send.at[k, s], rows_recv.at[k, s],
+                device_id=(ahead, s), device_id_type=MESH,
+            ).wait_recv()
+        upper = jnp.dot(order, rows_in[:, :, cut].reshape(every, piece), preferred_element_type=F32)
+        back_out[:, :, cut] = upper.astype(jnp.bfloat16).reshape(n_fsdp, block, piece)
+        for d in range(1, n_fsdp):
+            peer = lax.rem(f + d, n_fsdp)
+            copy = pltpu.make_async_remote_copy(
+                back_out.at[peer, :, cut], back_in.at[f, :, cut],
+                back_send.at[k, d - 1], back_recv.at[k, d - 1],
+                device_id=(g, peer), device_id_type=MESH,
+            )
+            copy.start()
+            back_copies.append(copy)
+        value = vis_in[:, :, cut].reshape(every, piece).astype(F32)
+        share_terms[:, cut] = jnp.sum(upper * value * inv_all, axis=0, keepdims=True)
+    second[g] = part + share_terms[...]
 
     def send(d, carry):
         peer = lax.rem(g + d, n_grp)
@@ -261,7 +284,33 @@
         return carry
 
     lax.fori_loop(1, n_grp, send, 0)
-    for copy in slot_copies + row_copies + first_copies:
+    back_in[f] = back_out[f]
+    for k in range(PIECES):
+        for d in range(1, n_fsdp):
+            source = lax.rem(f + n_fsdp - d, n_fsdp)
+            cut = slice(k * piece, (k + 1) * piece)
+            pltpu.make_async_remote_copy(
+                back_in.at[source, :, cut], back_in.at[source, :, cut],
+                back_send.at[k, d - 1], back_recv.at[k, d - 1],
+                device_id=(g, source), device_id_type=MESH,
+            ).wait_recv()
+    inner = jnp.zeros((block, LANES), F32)
+    for q in range(n_fsdp):
+        for k in range(PIECES):
+            cut = slice(k * piece, (k + 1) * piece)
+            product = back_in[q, :, cut].astype(F32) * vis_out[q, :, cut].astype(F32) * gain_rows[q][k]
+            for c in range(0, piece, LANES):
+                inner += product[:, c : c + LANES]
+    inner = jnp.sum(inner, axis=1, keepdims=True) / width
+    factor = inv_vision * inv_vision * inv_vision * inner
+    for q in range(n_fsdp):
+        for k in range(PIECES):
+            cut = slice(k * piece, (k + 1) * piece)
+            scaled = back_in[q, :, cut].astype(F32) * gain_rows[q][k]
+            grad = (inv_vision * scaled - vis_out[q, :, cut].astype(F32) * factor).astype(jnp.bfloat16)
+            at = q * share + k * piece
+            grad_ref[:, at : at + piece] = jnp.dot(scatter, grad, preferred_element_type=F32).astype(jnp.bfloat16)
+    for copy in slot_copies + row_copies + first_copies + vis_copies + back_copies:
         copy.wait_send()
     lax.fori_loop(1, n_grp, arrive, 0)
     whole = second[0]
@@ -300,8 +349,13 @@
             vmem((n_fsdp, share // LANES, LANES), bf16),
             vmem((n_fsdp, block, share), bf16),
             vmem((n_fsdp, block, share), bf16),
-            vmem((vis_dev, width), F32),
             vmem((8, width), F32),
+            vmem((n_fsdp, block, share), bf16),
+            vmem((n_fsdp, block, share), bf16),
+            vmem((n_fsdp, block, LANES), F32),
+            vmem((n_fsdp, block, share), bf16),
+            vmem((n_fsdp, block, share), bf16),
+            vmem((1, share), F32),
             vmem((n_fsdp, 1, share), F32),
             vmem((n_fsdp - 1, 1, share), F32),
             vmem((n_grp, 1, share), F32),
@@ -312,6 +366,12 @@
             dma((n_fsdp - 1,)),
             dma((PIECES, n_fsdp)),
             dma((PIECES, n_fsdp)),
+            dma((n_fsdp - 1,)),
+            dma((n_fsdp - 1,)),
+            dma((n_fsdp - 1,)),
+            dma((n_fsdp - 1,)),
+            dma((PIECES, n_fsdp - 1)),
+            dma((PIECES, n_fsdp - 1)),
             dma((n_fsdp - 1,)),
             dma((n_fsdp - 1,)),
             dma((n_grp,)),

time: 27.5 us -> 25.8 us (0.938); the launches traced: 27.4 us -> 25.4 us
  Pallas kernels: 25.4 us -> 23.4 us
    pallas_call x1, Pallas kernels: 25.4 us -> 23.4 us  [shards(): pl.pallas_call(functools.partial(kernel, n_grp, n_fsdp, hop, capacity), o...]
where the time goes in v4:
time: 25.8 us; the launch traced here: 25.4 us
  Pallas kernels  23.4 us (91%)
  local copies, waits for them, and re-layouts  1.3 us (5%)
  between operations  0.64 us (2%)
    pallas_call x1, Pallas kernels, shards(): pl.pallas_call(functools.partial(kernel, n_grp, n_fsdp, hop, capacity), o...  23.4 us
    unnamed x2, local copies, waits for them, and re-layouts  1.3 us

profile of v4, /device:TPU:0, one launch (start us, length us, event | category | flops | bytes accessed | tf_op | source)
XLA Modules:
  0.0 25.4 jit_solution(5681082198214945783)
XLA Ops:
  0.6 23.4 %shard_map.68 = (bf16[16,8192]{1,0:T(8,128)(2,1)S(1)}, f32[1,2048]{1,0:T(1,128)S(1)}) custom-call(s32[1,16]{1,0:T(1,128)} %bitcast.5, bf16[16,128]{1,0:T(8,128)(2,1)} %bitcast.4, bf16[16,8192]{1,0:T(8,128)(2,1)} %vision_hbm.1, bf16[128,8192]{1,0:T(8,128)(2,1)} %text_hbm.1, bf16[128,8192]{1,0:T(8,128)(2,1)} %cot_hbm.1), custom_call_target="tpu_custom_call" | custom-call | tf_op jit(solution)/shard_map/pallas_call | solution.py:334
  24.1 0.7 %copy.9 = bf16[16,8192]{1,0:T(8,128)(2,1)} copy(bf16[16,8192]{1,0:T(8,128)(2,1)S(1)} %get-tuple-element.8) | data formatting | bytes 524288
  24.8 0.6 %copy.10 = f32[2048]{0:T(1024)} copy(f32[2048]{0:T(1024)S(1)} %bitcast.3) | data formatting | bytes 16384
